TPU v7x, 32 devices: a whole 2x2x4 slice. The times are simulated.
32 devices in a mesh: grp: 2 (over y), row: 4 (over z), col: 4 (over x, core).
Axes of the slice: x: 2, y: 2, z: 4, core: 2. Of those that a mesh axis runs over, the one named last changes fastest.
Arguments:
- pair: bfloat16 [128, 64, 128], P(('grp', 'row'), 'col'), parts along dimension 0, may hold values from -6 to 6
- cotangent: bfloat16 [128, 64, 128], P(('grp', 'row'), 'col'), parts along dimension 0, may hold values from -6 to 6
- weight_codes: int32 [6, 128, 128], replicated, may hold values from -127 to 127
- exponents: int32 [6, 4], replicated, may hold values from -11 to -9
- residue_mask: int32 [128], P('grp'), parts along dimension 0, may hold values 0 or 1
Outputs:
- pair_grad: float32 [128, 64, 128], P(('grp', 'row'), 'col'), parts along dimension 0
There are 2 independent parts, one for each index of `grp`. A program takes and returns all parts, laid end to end along the dimension named above; an argument that names none is the same for every part. Nothing has to cross between parts.
All inputs are finite; a program needn't handle non-finite values.
Results may differ from a plain program's by a relative error of at most 0.012.
Values may be sent and summed in bfloat16 or wider, within the bound.
A program may use at most 64 MiB of HBM per device.

v0:
```python
import jax
import jax.numpy as jnp
from jax import lax
from jax.sharding import PartitionSpec as P


def layer_norm(values):
    average = jnp.mean(values, axis=-1, keepdims=True)
    centered = values - average
    inverse = lax.rsqrt(jnp.mean(centered * centered, axis=-1, keepdims=True) + 1e-05)
    return (centered * inverse, inverse)


def norm_back(normed, inverse, upstream):
    first = jnp.mean(upstream, axis=-1, keepdims=True)
    second = jnp.mean(upstream * normed, axis=-1, keepdims=True)
    return inverse * (upstream - first - normed * second)


def restore_weights(weight_codes, exponents):
    matrices = weight_codes.shape[0]
    width = weight_codes.shape[1]
    blocks = exponents.shape[1]
    factor = jnp.exp2(exponents.astype(jnp.float32))[:, :, None, None]
    scaled = (
        weight_codes.astype(jnp.float32).reshape(matrices, blocks, width // blocks, width) * factor
    )
    return scaled.reshape(matrices, width, width).astype(jnp.bfloat16)


def per_device(pair, cotangent, weight_codes, exponents, residue_mask):
    tile_rows = pair.shape[0]
    width = pair.shape[2]
    weights = restore_weights(weight_codes, exponents)
    stacked = jnp.concatenate([weights[0], weights[1], weights[2], weights[3], weights[4]], axis=1)
    row_start = lax.axis_index("row") * tile_rows
    col_start = lax.axis_index("col") * tile_rows
    row_keep = lax.dynamic_slice_in_dim(residue_mask, row_start, tile_rows).astype(jnp.float32)
    col_keep = lax.dynamic_slice_in_dim(residue_mask, col_start, tile_rows).astype(jnp.float32)
    pair_mask = (row_keep[:, None] * col_keep[None, :])[:, :, None]
    normed, inverse = layer_norm(pair.astype(jnp.float32))
    pair_normed = normed.astype(jnp.bfloat16)
    projected = jnp.dot(pair_normed.reshape(-1, width), stacked, preferred_element_type=jnp.float32)
    projected = projected.reshape(tile_rows, tile_rows, 5 * width)
    left_gate = projected[:, :, 0:width]
    left_value = projected[:, :, width : 2 * width]
    right_gate = projected[:, :, 2 * width : 3 * width]
    right_value = projected[:, :, 3 * width : 4 * width]
    out_gate = projected[:, :, 4 * width : 5 * width]
    left_sigmoid = jax.nn.sigmoid(left_gate)
    right_sigmoid = jax.nn.sigmoid(right_gate)
    left_tile = (pair_mask * left_sigmoid * left_value).astype(jnp.bfloat16)
    right_tile = (pair_mask * right_sigmoid * right_value).astype(jnp.bfloat16)
    right_strip = lax.all_gather(right_tile, "row", axis=0, tiled=True)
    window = right_strip
    swapped = lax.psum_scatter(
        jnp.einsum("jkc,ikc->jic", window, left_tile, preferred_element_type=jnp.float32).astype(
            jnp.bfloat16
        ),
        "col",
        scatter_dimension=0,
        tiled=True,
    ).astype(jnp.float32)
    update = jnp.transpose(swapped, (1, 0, 2))
    update_normed, update_inverse = layer_norm(update)
    out_value = jnp.dot(
        update_normed.astype(jnp.bfloat16).reshape(-1, width),
        weights[5],
        preferred_element_type=jnp.float32,
    )
    out_value = out_value.reshape(tile_rows, tile_rows, width)
    gate = jax.nn.sigmoid(out_gate)
    upstream = cotangent.astype(jnp.float32)
    grad_value = (upstream * gate).astype(jnp.bfloat16)
    grad_gate = (upstream * out_value * gate * (1.0 - gate)).astype(jnp.bfloat16)
    grad_normed = jnp.dot(
        grad_value.reshape(-1, width), weights[5].T, preferred_element_type=jnp.float32
    )
    grad_normed = grad_normed.reshape(tile_rows, tile_rows, width)
    update_grad = norm_back(update_normed, update_inverse, grad_normed).astype(jnp.bfloat16)
    update_strip = lax.all_gather(update_grad, "col", axis=1, tiled=True)
    right_again = lax.all_gather(right_tile, "row", axis=0, tiled=True)
    left_grad = jnp.einsum(
        "ijc,jkc->ikc", update_strip, right_again, preferred_element_type=jnp.float32
    )
    window = update_strip
    right_grad = lax.psum_scatter(
        jnp.einsum("ijc,ikc->jkc", window, left_tile, preferred_element_type=jnp.float32).astype(
            jnp.bfloat16
        ),
        "row",
        scatter_dimension=0,
        tiled=True,
    ).astype(jnp.float32)
    left_gate_grad = (
        left_grad * pair_mask * left_value * left_sigmoid * (1.0 - left_sigmoid)
    ).astype(jnp.bfloat16)
    left_value_grad = (left_grad * pair_mask * left_sigmoid).astype(jnp.bfloat16)
    right_gate_grad = (
        right_grad * pair_mask * right_value * right_sigmoid * (1.0 - right_sigmoid)
    ).astype(jnp.bfloat16)
    right_value_grad = (right_grad * pair_mask * right_sigmoid).astype(jnp.bfloat16)
    joined = jnp.concatenate(
        [left_gate_grad, left_value_grad, right_gate_grad, right_value_grad, grad_gate], axis=-1
    )
    normed_grad = jnp.dot(
        joined.reshape(-1, 5 * width), stacked.T, preferred_element_type=jnp.float32
    )
    normed_grad = normed_grad.reshape(tile_rows, tile_rows, width)
    return norm_back(normed, inverse, normed_grad)


def solution(mesh):
    in_specs = (P(("grp", "row"), "col", None), P(("grp", "row"), "col", None), P(), P(), P("grp"))
    out_specs = P(("grp", "row"), "col", None)
    return jax.shard_map(
        per_device, mesh=mesh, in_specs=in_specs, out_specs=out_specs, check_vma=False
    )
```

profile of v0, /device:TPU:0, one launch (start us, length us, event | category | flops | bytes accessed | tf_op | source)
XLA Modules:
  0.0 92.5 jit_solution(3668856026628591722)
XLA Ops:
  6.5 0.7 copy-done.6
  7.2 0.1 copy.15
  7.3 0.1 mul.177
  7.4 0.1 mul.178
  7.5 1.2 %multiply_convert_fusion = bf16[6,128,128]{2,1,0:T(8,128)(2,1)S(1)} fusion(s32[6,128,128]{2,1,0:T(8,128)} %param.7, f32[6,128]{1,0:T(8,128)S(1)} %mul.178), kind=kLoop, calls=%fused_computation.7 | loop fusion | flops 294912 | bytes 592896 | tf_op jit(solution)/shard_map/convert_element_type | solution.py:28
  8.7 0.0 copy-start
  8.8 0.8 copy-done
  9.6 0.1 convert_reduce_fusion
  9.7 0.2 fusion.17
  9.9 0.3 fusion.7
  10.2 0.0 copy-start.5
  10.2 0.6 copy-done.5
  10.9 0.1 dynamic-slice_convert_fusion.1
  11.0 0.1 broadcast_multiply_fusion
  11.0 0.1 multiply_convert_fusion.5
  11.1 15.6 %all_gather.7 = bf16[64,16,128]{2,1,0:T(8,128)(2,1)S(1)} all-gather(bf16[16,16,128]{2,1,0:T(8,128)(2,1)S(1)} %get-tuple-element.10), channel_id=1, replica_groups=mesh['grp'=2,'row'=4,'col'=4] {'row'}, dimensions={0}, use_global_device_ids=true | all-gather | bytes 327680 | tf_op jit(solution)/shard_map/all_gather | solution.py:82
  26.8 0.5 copy.21
  27.3 0.4 copy.24
  27.8 0.4 fusion
  28.1 1.3 %copy.18 = bf16[64,16,128]{2,1,0:T(8,128)(2,1)} copy(bf16[64,16,128]{0,1,2:T(8,128)(2,1)S(1)} %fusion) | data formatting | bytes 524288 | tf_op jit(solution)/shard_map/convert_element_type | solution.py:57
  29.4 0.0 reduce-scatter.3.cloned.1.call-update
  29.4 0.0 reduce-scatter.5.cloned.1.call-start
  29.5 21.7 %reduce-scatter.3.cloned.1.call-done = bf16[16,16,128]{2,1,0:T(8,128)(2,1)} async-done(((bf16[64,16,128]{2,1,0:T(8,128)(2,1)}), bf16[16,16,128]{2,1,0:T(8,128)(2,1)}) %reduce-scatter.3.cloned.1.call-update) | async-done | bytes 65552 | tf_op jit(solution)/shard_map/reduce_scatter | solution.py:56
  51.1 1.0 %bitcast_reduce_fusion = f32[16,16]{1,0:T(8,128)S(1)} fusion(bf16[16,16,128]{2,1,0:T(8,128)(2,1)} %reduce-scatter.3.cloned.1.call-done), kind=kLoop, calls=%fused_computation.40 | loop fusion | flops 65280 | bytes 66560 | tf_op jit(solution)/shard_map/reduce_sum | solution.py:8
  52.1 0.0 copy-start.7
  52.2 0.2 fusion.37
  52.4 0.0 copy-done.1
  52.4 0.6 copy-done.7
  53.0 0.3 fusion.59
  53.3 0.2 fusion.36
  53.5 5.8 %all_gather.8 = bf16[16,64,128]{2,0,1:T(8,128)(2,1)S(1)} all-gather(bf16[16,16,128]{2,0,1:T(8,128)(2,1)S(1)} %copy.20), channel_id=1, replica_groups=mesh['grp'=2,'row'=4,'col'=4] {'col'}, dimensions={1}, use_global_device_ids=true | all-gather | bytes 327680 | tf_op jit(solution)/shard_map/all_gather | solution.py:81
  59.3 0.5 copy.22
  59.9 0.4 fusion.61
  60.3 1.3 %copy.26 = bf16[128,16,64]{0,1,2:T(8,128)(2,1)} copy(bf16[128,16,64]{2,1,0:T(8,128)(2,1)S(1)} %fusion.61) | data formatting | bytes 524288 | tf_op jit(solution)/shard_map/ijc,ikc->jkc/dot_general | solution.py:88
  61.5 0.0 reduce-scatter.5.cloned.1.call-update
  61.6 0.4 fusion.60
  61.9 0.4 copy.23
  62.4 0.1 fusion.38
  62.5 0.1 fusion.39
  62.6 18.8 %reduce-scatter.5.cloned.1.call-done = bf16[16,16,128]{2,1,0:T(8,128)(2,1)} async-done(((bf16[64,16,128]{2,1,0:T(8,128)(2,1)}), bf16[16,16,128]{2,1,0:T(8,128)(2,1)}) %reduce-scatter.5.cloned.1.call-update) | async-done | bytes 65552 | tf_op jit(solution)/shard_map/reduce_scatter | solution.py:87
  81.4 1.0 %fusion.40 = bf16[16,16,640]{2,1,0:T(8,128)(2,1)S(1)} fusion(bf16[16,16,640]{2,1,0:T(8,128)(2,1)S(1)} %fusion.39, f32[16,16,640]{2,1,0:T(8,128)S(1)} %fusion.7, bf16[16,16,128]{2,1,0:T(8,128)(2,1)} %reduce-scatter.5.cloned.1.call-done, f32[16,16]{1,0:T(8,128)S(1)} %broadcast_multiply_fusion), kind=kLoop, calls=%fused_computation.60 | loop fusion | flops 327680 | bytes 401408
  82.5 0.0 copy-start.8
  82.5 0.1 fusion.41
  82.6 0.7 copy-done.3
  83.3 0.0 copy-done.8
  83.3 1.0 %fusion.4 = bf16[16,16,640]{2,1,0:T(8,128)(2,1)S(1)} fusion(bf16[16,16,640]{2,1,0:T(8,128)(2,1)S(1)} %fusion.41, bf16[16,16,128]{2,1,0:T(8,128)(2,1)S(1)} %copy-done.8, f32[16,16]{1,0:T(8,128)S(1)} %add_rsqrt_fusion, f32[16,16]{1,0:T(8,128)S(1)} %broadcast_multiply_fusion.5, bf16[16,16,128]{2,1,0:T(8,128)(2,1)S(1)} %copy-done.3, ...), kind=kOutput, calls=%fused_computation.6 | convolution fusion | flops 8814592 | bytes 376832 | tf_op jit(solution)/shard_map/dot_general | solution.py:66
  84.4 0.4 fusion.58
  84.8 0.9 fusion.16
  (22 shorter events, 0.1 us)
Async XLA Ops:
  6.5 44.6 %reduce-scatter.3.cloned.1.call-start = ((), (), s32[]{:S(2)}) async-start(), calls=%async_computation.2 | async-start | bytes 327680 | tf_op jit(solution)/shard_map/reduce_scatter | solution.py:56
  6.5 0.7 copy-start.6
  8.7 43.7 %copy-start.1 = (bf16[6,128,128]{2,1,0:T(8,128)(2,1)}, bf16[6,128,128]{2,1,0:T(8,128)(2,1)S(1)}, u32[]{:S(2)}) copy-start(bf16[6,128,128]{2,1,0:T(8,128)(2,1)S(1)} %multiply_convert_fusion) | copy-start | bytes 589828
  8.7 0.9 copy-start
  10.2 0.7 copy-start.5
  29.4 52.0 %reduce-scatter.5.cloned.1.call-start = ((), (), s32[]{:S(2)}) async-start(), calls=%async_computation.3 | async-start | bytes 327680 | tf_op jit(solution)/shard_map/reduce_scatter | solution.py:87
  51.1 1.1 %copy-start.2 = (bf16[16,16,128]{2,1,0:T(8,128)(2,1)S(1)}, bf16[16,16,128]{2,1,0:T(8,128)(2,1)}, u32[]{:S(2)}) copy-start(bf16[16,16,128]{2,1,0:T(8,128)(2,1)} %reduce-scatter.3.cloned.1.call-done) | copy-start | bytes 196612
  52.1 0.8 copy-start.7
  81.4 1.0 %copy-start.4 = (bf16[16,16,128]{2,1,0:T(8,128)(2,1)S(1)}, bf16[16,16,128]{2,1,0:T(8,128)(2,1)}, u32[]{:S(2)}) copy-start(bf16[16,16,128]{2,1,0:T(8,128)(2,1)} %reduce-scatter.5.cloned.1.call-done) | copy-start | bytes 196612
  82.5 0.8 copy-start.3
  82.5 0.9 copy-start.8
Sparse Core Ops, SparseCore 0:
  29.5 21.5 reduce-scatter.2
  61.7 19.7 reduce-scatter.4
where the time goes:
time: 93 us; the launch traced here: 92.5 us
  waiting for transfers between devices  40.5 us (44%)
  blocking collectives  21.4 us (23%)
  between operations  13.7 us (15%)
  local copies, waits for them, and re-layouts  8.32 us (9%)
  other arithmetic  5.4 us (6%)
  matrix products  3.12 us (3%)
    reduce_scatter x1, waiting for transfers between devices, per_device(): lax.psum_scatter(jnp.einsum('jkc,ikc->jic', window, left_tile, preferred_...  21.7 us
    reduce_scatter x1, waiting for transfers between devices, per_device(): lax.psum_scatter(jnp.einsum('ijc,ikc->jkc', window, left_tile, preferred_...  18.8 us
    all_gather x1, blocking collectives, per_device(): right_again = lax.all_gather(right_tile, 'row', axis=0, tiled=True)  15.6 us
    all_gather x1, blocking collectives, per_device(): update_strip = lax.all_gather(update_grad, 'col', axis=1, tiled=True)  5.79 us
    unnamed x22, local copies, waits for them, and re-layouts  3.54 us
  transfers between devices with their start and end apart: 2, of which 2 were waited for; matrix products, arithmetic and copies ran while one was open for 1% of the time, Pallas kernels for 0%

commit v1 on v0

v1 whole, which is shorter than its diff:
```python
import functools

import jax
import jax.numpy as jnp
from jax import lax
from jax.experimental import pallas as pl
from jax.experimental.pallas import tpu as pltpu
from jax.sharding import PartitionSpec as P

F32 = jnp.float32
BF16 = jnp.bfloat16
MESH = pl.DeviceIdType.MESH
GROUP = 4


def partner(me, d, n):
    if n & (n - 1):
        return lax.rem(me + d, n)
    out = me
    bit = 1
    while bit < n:
        if d & bit:
            out = out + bit - 2 * bit * lax.rem(lax.div(me, bit), 2)
        bit *= 2
    return out


def dot(a, b):
    return jnp.dot(a, b, preferred_element_type=F32)


def dot_t(a, b):
    return lax.dot_general(a, b, (((1,), (1,)), ((), ())), preferred_element_type=F32)


def contract(side, rows_ref, row_base, outer, inner, mat_ref, mat_base, emit):
    def body(g, carry):
        first = g * GROUP
        sums = [None] * GROUP
        start = row_base + first * outer
        for s in range(side):
            block = mat_ref[pl.ds(mat_base + s * side, side), :]
            for q in range(GROUP):
                row = rows_ref[pl.ds(start + q * outer + s * inner, 1), :]
                term = row * block
                sums[q] = term if sums[q] is None else sums[q] + term
        for q in range(GROUP):
            emit(pl.multiple_of((first + q) * side, side), sums[q])
        return carry

    lax.fori_loop(0, side // GROUP, body, 0)


def kernel(side, n, pair_ref, cot_ref, codes_ref, exps_ref, mask_ref, out_ref,
           w_ref, perm_ref, rbuf, rf, ubuf, sbuf, cbuf, ugf, ebuf, gbuf,
           left_f, left_t, coef, keep, lg_ref, send_sem, recv_sem):
    rows = side * side
    width = pair_ref.shape[1]
    my_row = lax.axis_index("row")
    my_col = lax.axis_index("col")
    shift = side.bit_length() - 1

    barrier = pltpu.get_barrier_semaphore()
    for d in range(1, n):
        pl.semaphore_signal(barrier, inc=1, device_id={"row": partner(my_row, d, n)}, device_id_type=MESH)
        pl.semaphore_signal(barrier, inc=1, device_id={"col": partner(my_col, d, n)}, device_id_type=MESH)

    def remote(stage, src, dst, send_slot, recv_slot, target):
        return pltpu.make_async_remote_copy(
            src_ref=src, dst_ref=dst,
            send_sem=send_sem.at[stage, send_slot], recv_sem=recv_sem.at[stage, recv_slot],
            device_id=target, device_id_type=MESH,
        )

    def wait_arrival(stage, buf, slot, axis):
        remote(stage, buf.at[slot], buf.at[slot], 0, slot, {axis: slot}).wait_recv()

    factor = jnp.exp2(exps_ref[...].astype(F32))
    blocks = exps_ref.shape[1]
    depth = width // blocks

    def restore(m):
        for b in range(blocks):
            scaled = codes_ref[m, b * depth:(b + 1) * depth, :].astype(F32) * factor[m:m + 1, b:b + 1]
            w_ref[b * depth:(b + 1) * depth, m * width:(m + 1) * width] = scaled.astype(BF16)

    def weight(first, last):
        return w_ref[:, first * width:last * width]

    for m in (2, 3):
        restore(m)

    total = mask_ref.shape[1]
    at_row = lax.broadcasted_iota(jnp.int32, (rows, total), 0)
    at_lane = lax.broadcasted_iota(jnp.int32, (rows, total), 1)
    picks = jnp.where(at_lane == my_row * side + (at_row >> shift), 1.0, 0.0) + jnp.where(
        at_lane == my_col * side + (at_row & (side - 1)), 1.0, 0.0)
    kept = jnp.broadcast_to(mask_ref[...].astype(F32), (width, total)).astype(BF16)
    pair_mask = jnp.where(dot_t(picks.astype(BF16), kept) > 1.5, 1.0, 0.0)

    x = pair_ref[...].astype(F32)
    centered = x - jnp.mean(x, axis=-1, keepdims=True)
    pair_inverse = lax.rsqrt(jnp.mean(centered * centered, axis=-1, keepdims=True) + 1e-05)
    normed = centered * pair_inverse
    pair_normed = normed.astype(BF16)

    projected = dot(pair_normed, weight(2, 4))
    gate_r, value_r = projected[:, :width], projected[:, width:]
    sig_r = jax.nn.sigmoid(gate_r)
    masked_r = pair_mask * sig_r
    right = (masked_r * value_r).astype(BF16)
    rbuf[my_row] = right
    pl.semaphore_wait(barrier, 2 * (n - 1))
    for d in range(1, n):
        remote(0, rbuf.at[my_row], rbuf.at[my_row], d, my_row, {"row": partner(my_row, d, n)}).start()
    coef[2] = masked_r * value_r * (1.0 - sig_r)
    coef[3] = masked_r
    rf[pl.ds(pl.multiple_of(my_row * rows, rows), rows), :] = right.astype(F32)

    a = lax.broadcasted_iota(jnp.int32, (rows, rows), 0)
    b = lax.broadcasted_iota(jnp.int32, (rows, rows), 1)
    perm_ref[...] = jnp.where(b == ((a & (side - 1)) << shift) + (a >> shift), 1.0, 0.0).astype(BF16)
    for m in (0, 1, 4, 5):
        restore(m)
    projected = dot(pair_normed, weight(0, 2))
    gate_l, value_l = projected[:, :width], projected[:, width:]
    sig_l = jax.nn.sigmoid(gate_l)
    masked_l = pair_mask * sig_l
    left = (masked_l * value_l).astype(BF16)
    left_f[...] = left.astype(F32)
    left_t[...] = dot(perm_ref[...], left)
    coef[0] = masked_l * value_l * (1.0 - sig_l)
    coef[1] = masked_l

    gate = jax.nn.sigmoid(dot(pair_normed, weight(4, 5)))
    upstream = cot_ref[...].astype(F32)
    gated = upstream * gate
    keep[0] = gated * (1.0 - gate)
    grad_normed = dot_t(gated.astype(BF16), weight(5, 6))
    keep[1] = grad_normed - jnp.mean(grad_normed, axis=-1, keepdims=True)

    for d in range(n):
        r = partner(my_row, d, n)
        base = pl.multiple_of(r * rows, rows)
        if d > 0:
            wait_arrival(0, rbuf, r, "row")
            rf[pl.ds(base, rows), :] = rbuf[r].astype(F32)

        def emit(o, value, d=d):
            sbuf[d, pl.ds(o, side), :] = value.astype(BF16)

        contract(side, rf, base, side, 1, left_t, 0, emit)

        @pl.when(r != my_col)
        def _():
            remote(1, sbuf.at[d], ubuf.at[my_col], d, my_col, {"col": r}).start()

        @pl.when(r == my_col)
        def _():
            ubuf[my_col] = sbuf[d]

    for d in range(1, n):
        wait_arrival(1, ubuf, partner(my_col, d, n), "col")
    update = dot(perm_ref[...], ubuf[0])
    for s in range(1, n):
        update = update + dot(perm_ref[...], ubuf[s])

    centered = update - jnp.mean(update, axis=-1, keepdims=True)
    inverse = lax.rsqrt(jnp.mean(centered * centered, axis=-1, keepdims=True) + 1e-05)
    update_normed = centered * inverse
    grad_normed = keep[1]
    second = jnp.mean(grad_normed * update_normed, axis=-1, keepdims=True)
    update_grad = (inverse * (grad_normed - update_normed * second)).astype(BF16)
    cbuf[my_col] = update_grad
    for d in range(1, n):
        remote(2, cbuf.at[my_col], cbuf.at[my_col], d, my_col, {"col": partner(my_col, d, n)}).start()
    grad_gate = (keep[0] * dot(update_normed.astype(BF16), weight(5, 6))).astype(BF16)

    for d in range(n):
        c = partner(my_col, d, n)
        base = pl.multiple_of(c * rows, rows)
        if d > 0:
            wait_arrival(2, cbuf, c, "col")
        ugf[pl.ds(base, rows), :] = cbuf[c].astype(F32)

        def emit(o, value, d=d):
            ebuf[d, pl.ds(o, side), :] = value.astype(BF16)

        contract(side, ugf, base, 1, side, left_f, 0, emit)

        @pl.when(c != my_row)
        def _():
            remote(3, ebuf.at[d], gbuf.at[my_row], d, my_row, {"row": c}).start()

        @pl.when(c == my_row)
        def _():
            gbuf[my_row] = ebuf[d]

    for d in range(n):
        c = partner(my_col, d, n)
        base = pl.multiple_of(c * rows, rows)

        def emit(o, value, d=d):
            spot = (pl.ds(o, side), slice(None))
            lg_ref[spot] = value if d == 0 else lg_ref[spot] + value

        contract(side, ugf, base, side, 1, rf, base, emit)

    left_grad = lg_ref[...]
    normed_grad = (
        dot_t((left_grad * coef[0]).astype(BF16), weight(0, 1))
        + dot_t((left_grad * coef[1]).astype(BF16), weight(1, 2))
        + dot_t(grad_gate, weight(4, 5))
    )

    for d in range(1, n):
        wait_arrival(3, gbuf, partner(my_row, d, n), "row")
    right_grad = gbuf[0].astype(F32)
    for s in range(1, n):
        right_grad = right_grad + gbuf[s].astype(F32)
    normed_grad = (
        normed_grad
        + dot_t((right_grad * coef[2]).astype(BF16), weight(2, 3))
        + dot_t((right_grad * coef[3]).astype(BF16), weight(3, 4))
    )
    first = jnp.mean(normed_grad, axis=-1, keepdims=True)
    second = jnp.mean(normed_grad * normed, axis=-1, keepdims=True)
    out_ref[...] = pair_inverse * (normed_grad - first - normed * second)

    for d in range(1, n):
        remote(0, rbuf.at[my_row], rbuf.at[my_row], d, my_row, {"row": partner(my_row, d, n)}).wait_send()
        remote(2, cbuf.at[my_col], cbuf.at[my_col], d, my_col, {"col": partner(my_col, d, n)}).wait_send()
    for d in range(n):
        r = partner(my_row, d, n)
        c = partner(my_col, d, n)

        @pl.when(r != my_col)
        def _():
            remote(1, sbuf.at[d], ubuf.at[my_col], d, my_col, {"col": r}).wait_send()

        @pl.when(c != my_row)
        def _():
            remote(3, ebuf.at[d], gbuf.at[my_row], d, my_row, {"row": c}).wait_send()


def per_device(n, pair, cotangent, weight_codes, exponents, residue_mask):
    side = pair.shape[0]
    width = pair.shape[2]
    rows = side * side
    matrices = weight_codes.shape[0]
    slots = (n, rows, width)
    vmem = pl.BlockSpec(memory_space=pltpu.VMEM)
    out = pl.pallas_call(
        functools.partial(kernel, side, n),
        out_shape=jax.ShapeDtypeStruct((rows, width), F32),
        in_specs=[vmem] * 5,
        out_specs=vmem,
        scratch_shapes=[
            pltpu.VMEM((width, matrices * width), BF16),
            pltpu.VMEM((rows, rows), BF16),
            pltpu.VMEM(slots, BF16),
            pltpu.VMEM((n * rows, width), F32),
            pltpu.VMEM(slots, BF16),
            pltpu.VMEM(slots, BF16),
            pltpu.VMEM(slots, BF16),
            pltpu.VMEM((n * rows, width), F32),
            pltpu.VMEM(slots, BF16),
            pltpu.VMEM(slots, BF16),
            pltpu.VMEM((rows, width), F32),
            pltpu.VMEM((rows, width), F32),
            pltpu.VMEM((4, rows, width), F32),
            pltpu.VMEM((2, rows, width), F32),
            pltpu.VMEM((rows, width), F32),
            pltpu.SemaphoreType.DMA((4, n)),
            pltpu.SemaphoreType.DMA((4, n)),
        ],
        compiler_params=pltpu.CompilerParams(
            collective_id=0, has_side_effects=True, vmem_limit_bytes=40 * 1024 * 1024
        ),
    )(
        pair.reshape(rows, width),
        cotangent.reshape(rows, width),
        weight_codes,
        exponents,
        residue_mask.reshape(1, -1),
    )
    return out.reshape(pair.shape)


def solution(mesh):
    in_specs = (P(("grp", "row"), "col", None), P(("grp", "row"), "col", None), P(), P(), P("grp"))
    out_specs = P(("grp", "row"), "col", None)
    n = mesh.shape["row"]
    assert n == mesh.shape["col"]
    return jax.shard_map(
        functools.partial(per_device, n), mesh=mesh, in_specs=in_specs, out_specs=out_specs, check_vma=False
    )
```

time: 93 us -> 29.1 us (0.31)
  the two profiles are of different devices: /device:TPU:0 before, /device:TPU:3 now
where the time goes in v1:
time: 29.1 us; the launch traced here: 28.7 us
  Pallas kernels  24 us (82%)
  local copies, waits for them, and re-layouts  4.67 us (16%)
    pallas_call x1, Pallas kernels, per_device(): pl.pallas_call(functools.partial(kernel, side, n), out_shape=jax.ShapeDty...  24 us
    unnamed x12, local copies, waits for them, and re-layouts  4.67 us

profile of v1, /device:TPU:3, one launch (start us, length us, event | category | flops | bytes accessed | tf_op | source)
XLA Modules:
  0.0 28.7 jit_solution(11613671302573367965)
XLA Ops:
  0.0 0.0 copy-start.4
  0.0 0.7 %copy-done.4 = s32[6,4]{0,1:T(4,128)S(1)} copy-done((s32[6,4]{0,1:T(4,128)S(1)}, s32[6,4]{0,1:T(4,128)}, u32[]{:S(2)}) %copy-start.4) | copy-done | bytes 120
  0.7 0.0 copy-start.3
  0.7 0.1 copy.6.exps_ref
  0.8 0.6 %copy-done.3 = s32[64]{0:T(128)S(1)} copy-done((s32[64]{0:T(128)S(1)}, s32[64]{0:T(128)}, u32[]{:S(2)}) %copy-start.3) | copy-done | bytes 280
  1.3 0.0 copy-start
  1.3 1.0 %copy-done = s32[6,128,128]{2,1,0:T(8,128)S(1)} copy-done((s32[6,128,128]{2,1,0:T(8,128)S(1)}, s32[6,128,128]{2,1,0:T(8,128)}, u32[]{:S(2)}) %copy-start) | copy-done | bytes 393240
  2.3 0.0 copy-start.1
  2.3 0.8 %copy-done.1 = bf16[16,16,128]{2,1,0:T(8,128)(2,1)S(1)} copy-done((bf16[16,16,128]{2,1,0:T(8,128)(2,1)S(1)}, bf16[16,16,128]{2,1,0:T(8,128)(2,1)}, u32[]{:S(2)}) %copy-start.1) | copy-done | bytes 65560
  3.2 0.0 copy-start.2
  3.2 0.8 %copy-done.2 = bf16[16,16,128]{2,1,0:T(8,128)(2,1)S(1)} copy-done((bf16[16,16,128]{2,1,0:T(8,128)(2,1)S(1)}, bf16[16,16,128]{2,1,0:T(8,128)(2,1)}, u32[]{:S(2)}) %copy-start.2) | copy-done | bytes 65560
  4.0 24.0 %shard_map.55 = f32[256,128]{1,0:T(8,128)S(1)} custom-call(bf16[256,128]{1,0:T(8,128)(2,1)S(1)} %bitcast.5, bf16[256,128]{1,0:T(8,128)(2,1)S(1)} %bitcast.6, s32[6,128,128]{2,1,0:T(8,128)S(1)} %copy-done, s32[6,4]{1,0:T(8,128)S(1)} %copy.6.exps_ref, s32[1,64]{1,0:T(1,128)S(1)} %bitcast.7), custom_call_target="tpu_custom_call" | custom-call | tf_op jit(solution)/shard_map/pallas_call | solution.py:253
  28.0 0.7 %copy.8 = f32[16,16,128]{2,1,0:T(8,128)} copy(f32[16,16,128]{2,1,0:T(8,128)S(1)} %bitcast.4) | data formatting | bytes 262144
Async XLA Ops:
  0.0 0.7 %copy-start.4 = (s32[6,4]{0,1:T(4,128)S(1)}, s32[6,4]{0,1:T(4,128)}, u32[]{:S(2)}) copy-start(s32[6,4]{0,1:T(4,128)} %param.8) | copy-start | bytes 292
  0.7 0.7 %copy-start.3 = (s32[64]{0:T(128)S(1)}, s32[64]{0:T(128)}, u32[]{:S(2)}) copy-start(s32[64]{0:T(128)} %param.9) | copy-start | bytes 772
  1.3 1.0 %copy-start = (s32[6,128,128]{2,1,0:T(8,128)S(1)}, s32[6,128,128]{2,1,0:T(8,128)}, u32[]{:S(2)}) copy-start(s32[6,128,128]{2,1,0:T(8,128)} %codes_ref.1) | copy-start | bytes 1179652
  2.3 0.8 %copy-start.1 = (bf16[16,16,128]{2,1,0:T(8,128)(2,1)S(1)}, bf16[16,16,128]{2,1,0:T(8,128)(2,1)}, u32[]{:S(2)}) copy-start(bf16[16,16,128]{2,1,0:T(8,128)(2,1)} %param.5) | copy-start | bytes 196612
  3.2 0.8 %copy-start.2 = (bf16[16,16,128]{2,1,0:T(8,128)(2,1)S(1)}, bf16[16,16,128]{2,1,0:T(8,128)(2,1)}, u32[]{:S(2)}) copy-start(bf16[16,16,128]{2,1,0:T(8,128)(2,1)} %param.6) | copy-start | bytes 196612

commit v2 on v1

v2 whole, which is shorter than its diff:
```python
import functools

import jax
import jax.numpy as jnp
from jax import lax
from jax.experimental import pallas as pl
from jax.experimental.pallas import tpu as pltpu
from jax.sharding import PartitionSpec as P

F32 = jnp.float32
BF16 = jnp.bfloat16
MESH = pl.DeviceIdType.MESH
GROUP = 4
VMEM_LIMIT = 63 * 1024 * 1024


def partner(me, d, n):
    if n & (n - 1):
        return lax.rem(me + d, n)
    out = me
    bit = 1
    while bit < n:
        if d & bit:
            out = out + bit - 2 * bit * lax.rem(lax.div(me, bit), 2)
        bit *= 2
    return out


def dot(a, b):
    return jnp.dot(a, b, preferred_element_type=F32)


def dot_t(a, b):
    return lax.dot_general(a, b, (((1,), (1,)), ((), ())), preferred_element_type=F32)


def contract(side, rows_ref, row_base, outer, inner, mat_ref, mat_base, emit):
    def body(g, carry):
        first = g * GROUP
        sums = [None] * GROUP
        start = row_base + first * outer
        for s in range(side):
            block = mat_ref[pl.ds(mat_base + s * side, side), :]
            for q in range(GROUP):
                row = rows_ref[pl.ds(start + q * outer + s * inner, 1), :]
                term = row * block
                sums[q] = term if sums[q] is None else sums[q] + term
        for q in range(GROUP):
            emit(pl.multiple_of((first + q) * side, side), sums[q])
        return carry

    lax.fori_loop(0, side // GROUP, body, 0)


def kernel(side, n, pair_hbm, cot_hbm, codes_hbm, exps_hbm, mask_hbm, out_ref,
           pair_ref, cot_ref, codes_ref, exps_ref, mask_ref, load_sem, w_ref, perm_ref,
           own, rbuf, rf, lbuf, left_f, left_t, upd, cbuf, ugf, ebuf, gbuf, pbuf, hbuf,
           coef, keep, lg_ref, send_sem, recv_sem):
    rows = side * side
    width = pair_ref.shape[1]
    matrices = codes_ref.shape[0]
    loads = [
        pltpu.make_async_copy(src, dst, load_sem.at[i])
        for i, (src, dst) in enumerate([
            (pair_hbm, pair_ref),
            (codes_hbm.at[pl.ds(2, 2)], codes_ref.at[pl.ds(2, 2)]),
            (exps_hbm, exps_ref),
            (mask_hbm, mask_ref),
            (codes_hbm.at[pl.ds(0, 2)], codes_ref.at[pl.ds(0, 2)]),
            (codes_hbm.at[pl.ds(4, matrices - 4)], codes_ref.at[pl.ds(4, matrices - 4)]),
            (cot_hbm, cot_ref),
        ])
    ]
    for load in loads:
        load.start()
    my_row = lax.axis_index("row")
    my_col = lax.axis_index("col")
    shift = side.bit_length() - 1

    diagonal = my_row == my_col
    elsewhere = jnp.logical_not(diagonal)
    barrier = pltpu.get_barrier_semaphore()

    def greet(target):
        pl.semaphore_signal(barrier, inc=1, device_id=target, device_id_type=MESH)

    for d in range(1, n):
        greet({"row": partner(my_row, d, n)})
        greet({"col": partner(my_col, d, n)})
        greet({"row": my_col, "col": partner(my_col, d, n)})

    @pl.when(elsewhere)
    def _():
        greet({"row": my_col, "col": my_col})

    def remote(stage, src, dst, send_slot, recv_slot, target):
        return pltpu.make_async_remote_copy(
            src_ref=src, dst_ref=dst,
            send_sem=send_sem.at[stage, send_slot], recv_sem=recv_sem.at[stage, recv_slot],
            device_id=target, device_id_type=MESH,
        )

    def wait_arrival(stage, buf, slot, axis):
        remote(stage, buf.at[slot], buf.at[slot], 0, slot, {axis: slot}).wait_recv()

    for load in loads[:4]:
        load.wait()

    factor = jnp.exp2(exps_ref[...].astype(F32))
    blocks = exps_ref.shape[0]
    depth = width // blocks

    def restore(m):
        for b in range(blocks):
            scaled = codes_ref[m, b * depth:(b + 1) * depth, :].astype(F32) * factor[b:b + 1, m:m + 1]
            w_ref[b * depth:(b + 1) * depth, m * width:(m + 1) * width] = scaled.astype(BF16)

    def weight(first, last):
        return w_ref[:, first * width:last * width]

    for m in (2, 3):
        restore(m)

    total = mask_ref.shape[1]
    at_row = lax.broadcasted_iota(jnp.int32, (rows, total), 0)
    at_lane = lax.broadcasted_iota(jnp.int32, (rows, total), 1)
    picks = jnp.where(at_lane == my_row * side + (at_row >> shift), 1.0, 0.0) + jnp.where(
        at_lane == my_col * side + (at_row & (side - 1)), 1.0, 0.0)
    kept = jnp.broadcast_to(mask_ref[...].astype(F32), (width, total)).astype(BF16)
    pair_mask = jnp.where(dot_t(picks.astype(BF16), kept) > 1.5, 1.0, 0.0)

    x = pair_ref[...].astype(F32)
    centered = x - jnp.mean(x, axis=-1, keepdims=True)
    pair_inverse = lax.rsqrt(jnp.mean(centered * centered, axis=-1, keepdims=True) + 1e-05)
    normed = centered * pair_inverse
    pair_normed = normed.astype(BF16)

    projected = dot(pair_normed, weight(2, 4))
    gate_r, value_r = projected[:, :width], projected[:, width:]
    sig_r = jax.nn.sigmoid(gate_r)
    masked_r = pair_mask * sig_r
    right = (masked_r * value_r).astype(BF16)
    own[...] = right

    @pl.when(elsewhere)
    def _():
        pl.semaphore_wait(barrier, 3 * (n - 1) + 1)

    @pl.when(diagonal)
    def _():
        pl.semaphore_wait(barrier, 3 * (n - 1))

    def send_right(d):
        return remote(0, own, rbuf.at[my_col], d, my_col, {"row": partner(my_row, d, n), "col": my_row})

    for d in reversed(range(1, n)):
        send_right(d).start()

    @pl.when(elsewhere)
    def _():
        send_right(0).start()

    @pl.when(diagonal)
    def _():
        rbuf[my_col] = right

    coef[2] = masked_r * value_r * (1.0 - sig_r)
    coef[3] = masked_r

    a = lax.broadcasted_iota(jnp.int32, (rows, rows), 0)
    b = lax.broadcasted_iota(jnp.int32, (rows, rows), 1)
    perm_ref[...] = jnp.where(b == ((a & (side - 1)) << shift) + (a >> shift), 1.0, 0.0).astype(BF16)
    loads[4].wait()
    for m in (0, 1):
        restore(m)
    projected = dot(pair_normed, weight(0, 2))
    gate_l, value_l = projected[:, :width], projected[:, width:]
    sig_l = jax.nn.sigmoid(gate_l)
    masked_l = pair_mask * sig_l
    left = (masked_l * value_l).astype(BF16)
    lbuf[my_col] = left

    def send_left(d):
        return remote(4, lbuf.at[my_col], lbuf.at[my_col], d, my_col, {"col": partner(my_col, d, n)})

    for d in reversed(range(1, n)):
        send_left(d).start()
    left_f[...] = left.astype(F32)
    coef[0] = masked_l * value_l * (1.0 - sig_l)
    coef[1] = masked_l

    for load in loads[5:]:
        load.wait()
    for m in (4, 5):
        restore(m)
    swapped = dot(perm_ref[...], pair_normed).astype(BF16)
    gate = jax.nn.sigmoid(dot(swapped, weight(4, 5)))
    upstream = dot(perm_ref[...], cot_ref[...])
    gated = upstream * gate
    keep[0] = gated * (1.0 - gate)
    grad_normed = dot_t(gated.astype(BF16), weight(5, 6))
    keep[1] = grad_normed - jnp.mean(grad_normed, axis=-1, keepdims=True)

    for d in range(n):
        c = partner(my_col, d, n)
        base = pl.multiple_of(c * rows, rows)
        if d > 0:
            wait_arrival(4, lbuf, c, "col")
        left_t[...] = dot(perm_ref[...], lbuf[c])
        if d > 0:
            wait_arrival(0, rbuf, c, "col")
        else:

            @pl.when(elsewhere)
            def _():
                wait_arrival(0, rbuf, my_col, "row")

        rf[pl.ds(base, rows), :] = rbuf[c].astype(F32)

        def emit(o, value, d=d):
            spot = (pl.ds(o, side), slice(None))
            upd[spot] = value if d == 0 else upd[spot] + value

        contract(side, rf, base, side, 1, left_t, 0, emit)

    update = upd[...]
    centered = update - jnp.mean(update, axis=-1, keepdims=True)
    inverse = lax.rsqrt(jnp.mean(centered * centered, axis=-1, keepdims=True) + 1e-05)
    update_normed = centered * inverse
    grad_normed = keep[1]
    second = jnp.mean(grad_normed * update_normed, axis=-1, keepdims=True)
    update_grad = (inverse * (grad_normed - update_normed * second)).astype(BF16)
    cbuf[my_col] = update_grad

    def send_update(d):
        return remote(2, cbuf.at[my_col], cbuf.at[my_col], d, my_col, {"col": partner(my_col, d, n)})

    for d in range(1, n):
        send_update(d).start()

    def send_grad(d):
        return remote(3, ebuf.at[d], gbuf.at[my_row], d, my_row, {"row": partner(my_col, d, n)})

    def send_left_grad(d):
        return remote(1, pbuf.at[d], hbuf.at[my_col], d, my_col, {"col": partner(my_col, d, n)})

    def right_part(d):
        c = partner(my_col, d, n)
        base = pl.multiple_of(c * rows, rows)
        if d > 0:
            wait_arrival(2, cbuf, c, "col")
        ugf[pl.ds(base, rows), :] = cbuf[c].astype(F32)

        def emit(o, value):
            ebuf[d, pl.ds(o, side), :] = value.astype(BF16)

        contract(side, ugf, base, side, 1, left_f, 0, emit)

        @pl.when(c != my_row)
        def _():
            send_grad(d).start()

        @pl.when(c == my_row)
        def _():
            gbuf[my_row] = ebuf[d]

    own_base = pl.multiple_of(my_col * rows, rows)

    def left_part(d):
        c = partner(my_col, d, n)

        def emit(o, value):
            if d == 0:
                lg_ref[pl.ds(o, side), :] = value
            else:
                pbuf[d, pl.ds(o, side), :] = value.astype(BF16)

        contract(side, ugf, own_base, 1, side, rf, pl.multiple_of(c * rows, rows), emit)
        if d > 0:
            send_left_grad(d).start()

    right_part(0)
    for d in reversed(range(1, n)):
        left_part(d)
    right_part(1)
    left_part(0)
    for d in range(2, n):
        right_part(d)

    grad_gate = keep[0] * dot(update_normed.astype(BF16), weight(5, 6))
    grad_gate = dot(perm_ref[...], grad_gate.astype(BF16)).astype(BF16)
    left_grad = lg_ref[...]
    for d in range(1, n):
        c = partner(my_col, d, n)
        wait_arrival(1, hbuf, c, "col")
        left_grad = left_grad + hbuf[c].astype(F32)
    normed_grad = (
        dot_t((left_grad * coef[0]).astype(BF16), weight(0, 1))
        + dot_t((left_grad * coef[1]).astype(BF16), weight(1, 2))
        + dot_t(grad_gate, weight(4, 5))
    )

    for d in range(1, n):
        wait_arrival(3, gbuf, partner(my_row, d, n), "row")
    right_grad = gbuf[0].astype(F32)
    for s in range(1, n):
        right_grad = right_grad + gbuf[s].astype(F32)
    normed_grad = (
        normed_grad
        + dot_t((right_grad * coef[2]).astype(BF16), weight(2, 3))
        + dot_t((right_grad * coef[3]).astype(BF16), weight(3, 4))
    )
    first = jnp.mean(normed_grad, axis=-1, keepdims=True)
    second = jnp.mean(normed_grad * normed, axis=-1, keepdims=True)
    out_ref[...] = pair_inverse * (normed_grad - first - normed * second)

    for d in range(1, n):
        send_right(d).wait_send()
        send_left(d).wait_send()
        send_update(d).wait_send()
        send_left_grad(d).wait_send()

    @pl.when(elsewhere)
    def _():
        send_right(0).wait_send()

    for d in range(n):

        @pl.when(partner(my_col, d, n) != my_row)
        def _():
            send_grad(d).wait_send()


def per_device(n, pair, cotangent, weight_codes, exponents, residue_mask):
    side = pair.shape[0]
    width = pair.shape[2]
    rows = side * side
    matrices = weight_codes.shape[0]
    slots = (n, rows, width)
    vmem = pl.BlockSpec(memory_space=pltpu.VMEM)
    out = pl.pallas_call(
        functools.partial(kernel, side, n),
        out_shape=jax.ShapeDtypeStruct((rows, width), F32),
        in_specs=[pl.BlockSpec(memory_space=pltpu.HBM)] * 5,
        out_specs=vmem,
        scratch_shapes=[
            pltpu.VMEM((rows, width), pair.dtype),
            pltpu.VMEM((rows, width), cotangent.dtype),
            pltpu.VMEM(weight_codes.shape, weight_codes.dtype),
            pltpu.VMEM(exponents.shape[::-1], exponents.dtype),
            pltpu.VMEM((1, residue_mask.shape[0]), residue_mask.dtype),
            pltpu.SemaphoreType.DMA((7,)),
            pltpu.VMEM((width, matrices * width), BF16),
            pltpu.VMEM((rows, rows), BF16),
            pltpu.VMEM((rows, width), BF16),
            pltpu.VMEM(slots, BF16),
            pltpu.VMEM((n * rows, width), F32),
            pltpu.VMEM(slots, BF16),
            pltpu.VMEM((rows, width), F32),
            pltpu.VMEM((rows, width), F32),
            pltpu.VMEM((rows, width), F32),
            pltpu.VMEM(slots, BF16),
            pltpu.VMEM((n * rows, width), F32),
            pltpu.VMEM(slots, BF16),
            pltpu.VMEM(slots, BF16),
            pltpu.VMEM(slots, BF16),
            pltpu.VMEM(slots, BF16),
            pltpu.VMEM((4, rows, width), F32),
            pltpu.VMEM((2, rows, width), F32),
            pltpu.VMEM((rows, width), F32),
            pltpu.SemaphoreType.DMA((5, n)),
            pltpu.SemaphoreType.DMA((5, n)),
        ],
        compiler_params=pltpu.CompilerParams(
            collective_id=0, has_side_effects=True, vmem_limit_bytes=VMEM_LIMIT
        ),
    )(
        pair.reshape(rows, width),
        cotangent.reshape(rows, width),
        weight_codes,
        exponents.T,
        residue_mask.reshape(1, -1),
    )
    return out.reshape(pair.shape)


def solution(mesh):
    in_specs = (P(("grp", "row"), "col", None), P(("grp", "row"), "col", None), P(), P(), P("grp"))
    out_specs = P(("grp", "row"), "col", None)
    n = mesh.shape["row"]
    assert n == mesh.shape["col"]
    return jax.shard_map(
        functools.partial(per_device, n), mesh=mesh, in_specs=in_specs, out_specs=out_specs, check_vma=False
    )
```

time: 29.1 us -> 25.6 us (0.88)
  local copies, waits for them, and re-layouts: 4.67 us -> 1.57 us
    unnamed x12 -> x1, local copies, waits for them, and re-layouts: 4.67 us -> 1.57 us
where the time goes in v2:
time: 25.6 us; the launch traced here: 25.4 us
  Pallas kernels  23.9 us (93%)
  local copies, waits for them, and re-layouts  1.57 us (6%)
    pallas_call x1, Pallas kernels, per_device(): pl.pallas_call(functools.partial(kernel, side, n), out_shape=jax.ShapeDty...  23.9 us
    unnamed x1, local copies, waits for them, and re-layouts  1.57 us

profile of v2, /device:TPU:3, one launch (start us, length us, event | category | flops | bytes accessed | tf_op | source)
XLA Modules:
  0.0 25.4 jit_solution(10606764015382735459)
XLA Ops:
  0.0 23.9 %shard_map.55 = f32[256,128]{1,0:T(8,128)} custom-call(bf16[256,128]{1,0:T(8,128)(2,1)} %bitcast.6, bf16[256,128]{1,0:T(8,128)(2,1)} %bitcast.7, s32[6,128,128]{2,1,0:T(8,128)} %codes_hbm.1, s32[4,6]{1,0:T(4,128)} %bitcast.8, s32[1,64]{1,0:T(1,128)} %bitcast.9), custom_call_target="tpu_custom_call" | custom-call | tf_op jit(solution)/shard_map/pallas_call | solution.py:341
  23.9 1.6 %copy.7 = f32[16,16,128]{2,1,0:T(8,128)} copy(f32[16,16,128]{2,1,0:T(8,128)} %bitcast.5) | data formatting | bytes 262144

commit v3 on v2

--- a/solution.py
+++ b/solution.py
@@ -10,7 +10,7 @@
 F32 = jnp.float32
 BF16 = jnp.bfloat16
 MESH = pl.DeviceIdType.MESH
-GROUP = 4
+GROUP = 8
 VMEM_LIMIT = 63 * 1024 * 1024
 
 
@@ -180,10 +180,16 @@
     left = (masked_l * value_l).astype(BF16)
     lbuf[my_col] = left
 
+    direct = [1] + list(range(2, n, 2))
+    sibling = {"col": partner(my_col, 1, n)}
+
     def send_left(d):
-        return remote(4, lbuf.at[my_col], lbuf.at[my_col], d, my_col, {"col": partner(my_col, d, n)})
-
-    for d in reversed(range(1, n)):
+        if d in direct:
+            return remote(4, lbuf.at[my_col], lbuf.at[my_col], d, my_col, {"col": partner(my_col, d, n)})
+        c = partner(my_col, d - 1, n)
+        return remote(4, lbuf.at[c], lbuf.at[c], d, c, sibling)
+
+    for d in direct:
         send_left(d).start()
     left_f[...] = left.astype(F32)
     coef[0] = masked_l * value_l * (1.0 - sig_l)
@@ -201,10 +207,14 @@
     grad_normed = dot_t(gated.astype(BF16), weight(5, 6))
     keep[1] = grad_normed - jnp.mean(grad_normed, axis=-1, keepdims=True)
 
+    for d in range(2, n, 2):
+        wait_arrival(4, lbuf, partner(my_col, d, n), "col")
+        send_left(d + 1).start()
+
     for d in range(n):
         c = partner(my_col, d, n)
         base = pl.multiple_of(c * rows, rows)
-        if d > 0:
+        if d % 2:
             wait_arrival(4, lbuf, c, "col")
         left_t[...] = dot(perm_ref[...], lbuf[c])
         if d > 0:
@@ -233,9 +243,12 @@
     cbuf[my_col] = update_grad
 
     def send_update(d):
-        return remote(2, cbuf.at[my_col], cbuf.at[my_col], d, my_col, {"col": partner(my_col, d, n)})
-
-    for d in range(1, n):
+        if d in direct:
+            return remote(2, cbuf.at[my_col], cbuf.at[my_col], d, my_col, {"col": partner(my_col, d, n)})
+        c = partner(my_col, d - 1, n)
+        return remote(2, cbuf.at[c], cbuf.at[c], d, c, sibling)
+
+    for d in direct:
         send_update(d).start()
 
     def send_grad(d):
@@ -247,7 +260,7 @@
     def right_part(d):
         c = partner(my_col, d, n)
         base = pl.multiple_of(c * rows, rows)
-        if d > 0:
+        if d % 2:
             wait_arrival(2, cbuf, c, "col")
         ugf[pl.ds(base, rows), :] = cbuf[c].astype(F32)
 
@@ -283,8 +296,12 @@
     for d in reversed(range(1, n)):
         left_part(d)
     right_part(1)
+    for d in range(2, n, 2):
+        wait_arrival(2, cbuf, partner(my_col, d, n), "col")
+        send_update(d + 1).start()
+    right_part(2)
     left_part(0)
-    for d in range(2, n):
+    for d in range(3, n):
         right_part(d)
 
     grad_gate = keep[0] * dot(update_normed.astype(BF16), weight(5, 6))
@@ -388,7 +405,7 @@
     in_specs = (P(("grp", "row"), "col", None), P(("grp", "row"), "col", None), P(), P(), P("grp"))
     out_specs = P(("grp", "row"), "col", None)
     n = mesh.shape["row"]
-    assert n == mesh.shape["col"]
+    assert n == mesh.shape["col"] and n & (n - 1) == 0
     return jax.shard_map(
         functools.partial(per_device, n), mesh=mesh, in_specs=in_specs, out_specs=out_specs, check_vma=False
     )

time: 25.6 us -> 25.3 us (0.988)
  Pallas kernels: 23.9 us -> 23.5 us
    pallas_call x1, Pallas kernels: 23.9 us -> 23.5 us  [per_device(): pl.pallas_call(functools.partial(kernel, side, n), out_shape=jax.ShapeDty...]
where the time goes in v3:
time: 25.3 us; the launch traced here: 25.1 us
  Pallas kernels  23.5 us (93%)
  local copies, waits for them, and re-layouts  1.57 us (6%)
    pallas_call x1, Pallas kernels, per_device(): pl.pallas_call(functools.partial(kernel, side, n), out_shape=jax.ShapeDty...  23.5 us
    unnamed x1, local copies, waits for them, and re-layouts  1.57 us

profile of v3, /device:TPU:3, one launch (start us, length us, event | category | flops | bytes accessed | tf_op | source)
XLA Modules:
  0.0 25.1 jit_solution(10271319240310054861)
XLA Ops:
  0.0 23.5 %shard_map.55 = f32[256,128]{1,0:T(8,128)} custom-call(bf16[256,128]{1,0:T(8,128)(2,1)} %bitcast.6, bf16[256,128]{1,0:T(8,128)(2,1)} %bitcast.7, s32[6,128,128]{2,1,0:T(8,128)} %codes_hbm.1, s32[4,6]{1,0:T(4,128)} %bitcast.8, s32[1,64]{1,0:T(1,128)} %bitcast.9), custom_call_target="tpu_custom_call" | custom-call | tf_op jit(solution)/shard_map/pallas_call | solution.py:358
  23.6 1.6 %copy.7 = f32[16,16,128]{2,1,0:T(8,128)} copy(f32[16,16,128]{2,1,0:T(8,128)} %bitcast.5) | data formatting | bytes 262144

commit v4 on v3

--- a/solution.py
+++ b/solution.py
@@ -293,16 +293,16 @@
             send_left_grad(d).start()
 
     right_part(0)
-    for d in reversed(range(1, n)):
+    for d in reversed(range(2, n)):
         left_part(d)
     right_part(1)
     for d in range(2, n, 2):
         wait_arrival(2, cbuf, partner(my_col, d, n), "col")
         send_update(d + 1).start()
-    right_part(2)
+    for d in range(2, n):
+        right_part(d)
+    left_part(1)
     left_part(0)
-    for d in range(3, n):
-        right_part(d)
 
     grad_gate = keep[0] * dot(update_normed.astype(BF16), weight(5, 6))
     grad_gate = dot(perm_ref[...], grad_gate.astype(BF16)).astype(BF16)

time: 25.3 us -> 25.3 us (level)
  no operation moved by 1% of the time
where the time goes in v4:
time: 25.3 us; the launch traced here: 25.1 us
  Pallas kernels  23.5 us (93%)
  local copies, waits for them, and re-layouts  1.57 us (6%)
    pallas_call x1, Pallas kernels, per_device(): pl.pallas_call(functools.partial(kernel, side, n), out_shape=jax.ShapeDty...  23.5 us
    unnamed x1, local copies, waits for them, and re-layouts  1.57 us

profile of v4, /device:TPU:3, one launch (start us, length us, event | category | flops | bytes accessed | tf_op | source)
XLA Modules:
  0.0 25.1 jit_solution(8304353907484017697)
XLA Ops:
  0.0 23.5 %shard_map.55 = f32[256,128]{1,0:T(8,128)} custom-call(bf16[256,128]{1,0:T(8,128)(2,1)} %bitcast.6, bf16[256,128]{1,0:T(8,128)(2,1)} %bitcast.7, s32[6,128,128]{2,1,0:T(8,128)} %codes_hbm.1, s32[4,6]{1,0:T(4,128)} %bitcast.8, s32[1,64]{1,0:T(1,128)} %bitcast.9), custom_call_target="tpu_custom_call" | custom-call | tf_op jit(solution)/shard_map/pallas_call | solution.py:358
  23.6 1.6 %copy.7 = f32[16,16,128]{2,1,0:T(8,128)} copy(f32[16,16,128]{2,1,0:T(8,128)} %bitcast.5) | data formatting | bytes 262144
